TPU v7x, 32 devices: a whole 2x2x4 slice. The times are simulated.
32 devices in a mesh: dp: 4 (over y, x), ctx: 8 (over z, core).
Axes of the slice: x: 2, y: 2, z: 4, core: 2. Of those that a mesh axis runs over, the one named last changes fastest.
Arguments:
- inputs: bfloat16 [4, 16, 65536], P('dp', None, 'ctx'), may hold values from -6 to 6
- out_grad: bfloat16 [4, 16, 65536], P('dp', None, 'ctx'), may hold values from -0.0625 to 0.0625
- master: float32 [16, 65536], P('ctx', 'dp'), may hold values from -0.0234375 to 0.0234375
- moment_one: float32 [16, 65536], P('ctx', 'dp'), may hold values from -6 to 6
- moment_two: float32 [16, 65536], P('ctx', 'dp'), may hold values from 0.05 to 1
- next_inputs: bfloat16 [4, 16, 65536], P('dp', None, 'ctx'), may hold values from -6 to 6
Outputs:
- new_master: float32 [16, 65536], P('ctx', 'dp')
- new_moment_one: float32 [16, 65536], P('ctx', 'dp')
- new_moment_two: float32 [16, 65536], P('ctx', 'dp')
- next_out: bfloat16 [4, 16, 65536], P('dp', None, 'ctx')
All inputs are finite; a program needn't handle non-finite values.
Results may differ from a plain program's by a relative error of at most 0.007.
Values may be sent and summed in bfloat16 or wider, within the bound.
A program may use at most 128 MiB of HBM per device.

v0:
```python
import math

import jax
import jax.numpy as jnp
from jax import lax
from jax.sharding import PartitionSpec as P

FA = 256


precise = lax.Precision.HIGH


def angles(rows, cols, period, row_start, col_start):
    row_ids = lax.broadcasted_iota(jnp.int32, (rows, cols), 0) + row_start
    col_ids = lax.broadcasted_iota(jnp.int32, (rows, cols), 1) + col_start
    phase = (row_ids * col_ids % period).astype(jnp.float32) * (2.0 * math.pi / period)
    return (jnp.cos(phase), jnp.sin(phase))


def mult(form, left, right):
    return jnp.einsum(form, left, right, precision=precise, preferred_element_type=jnp.float32)


def first_section(values, row_start, longer):
    cosine, sine = angles(longer, values.shape[1], longer, 0, row_start)
    real = mult("kr,crn->ckn", cosine, values)
    imag = -mult("kr,crn->ckn", sine, values)
    return (real, imag)


def second_section(real, imag):
    longer, inner = (real.shape[1], real.shape[2])
    tw_cos, tw_sin = angles(longer, inner, longer * inner, 0, 0)
    turned_re = real * tw_cos + imag * tw_sin
    turned_im = imag * tw_cos - real * tw_sin
    cosine, sine = angles(inner, inner, inner, 0, 0)
    out_re = mult("ckn,nm->ckm", turned_re, cosine) + mult("ckn,nm->ckm", turned_im, sine)
    out_im = mult("ckn,nm->ckm", turned_im, cosine) - mult("ckn,nm->ckm", turned_re, sine)
    return (out_re, out_im)


def back_section(spec_re, spec_im):
    longer, inner = (spec_re.shape[1], spec_re.shape[2])
    cosine, sine = angles(inner, inner, inner, 0, 0)
    mixed_re = mult("ckm,mn->ckn", spec_re, cosine) - mult("ckm,mn->ckn", spec_im, sine)
    mixed_im = mult("ckm,mn->ckn", spec_re, sine) + mult("ckm,mn->ckn", spec_im, cosine)
    tw_cos, tw_sin = angles(longer, inner, longer * inner, 0, 0)
    return (mixed_re * tw_cos - mixed_im * tw_sin, mixed_re * tw_sin + mixed_im * tw_cos)


def last_rows(back_re, back_im, start, count, form):
    longer, inner = (back_re.shape[1], back_re.shape[2])
    cosine, sine = angles(count, longer, longer, start, 0)
    total = mult(form, cosine, back_re) - mult(form, sine, back_im)
    return total * (1.0 / (longer * inner))


def spectrum(block, inner):
    channels, length = (block.shape[1], block.shape[2])
    values = block[0].reshape(channels, length // inner, inner)
    real, imag = first_section(values, 0, 2 * (length // inner))
    return second_section(real, imag)


def regroup_next(next_inputs):
    return lax.all_to_all(next_inputs, "ctx", split_axis=1, concat_axis=2, tiled=True)


def local(inputs, out_grad, master, moment_one, moment_two, next_inputs):
    inner = FA
    seq_local, grad_local = (
        lax.all_to_all(inputs, "ctx", split_axis=1, concat_axis=2, tiled=True),
        lax.all_to_all(out_grad, "ctx", split_axis=1, concat_axis=2, tiled=True),
    )
    channels, length = (seq_local.shape[1], seq_local.shape[2])
    half_rows = length // inner
    longer = 2 * half_rows
    seq_re, seq_im = spectrum(seq_local, inner)
    grad_re, grad_im = spectrum(grad_local, inner)
    prod_re = seq_re * grad_re + seq_im * grad_im
    prod_im = seq_re * grad_im - seq_im * grad_re
    back_re, back_im = back_section(prod_re, prod_im)
    rows_own = half_rows // lax.axis_size("dp")
    summed = lax.psum_scatter(
        last_rows(
            back_re, back_im, jnp.int32(0), lax.axis_size("dp") * rows_own, "rk,ckn->rcn"
        ).astype(jnp.bfloat16),
        "dp",
        scatter_dimension=0,
        tiled=True,
    ).astype(jnp.float32)
    grad = jnp.transpose(summed, (1, 0, 2)).reshape(channels, rows_own * inner)
    new_one = 0.9 * moment_one + 0.1 * grad
    new_two = 0.999 * moment_two + 0.001 * grad * grad
    first_hat = new_one / (1.0 - 0.9**10)
    second_hat = new_two / (1.0 - 0.999**10)
    new_master = master - 0.01 * (first_hat / (jnp.sqrt(second_hat) + 1e-08) + 0.1 * master)
    filters = new_master.astype(jnp.bfloat16).reshape(channels, rows_own, inner)
    part_re, part_im = first_section(
        lax.all_gather(filters, "dp", axis=1, tiled=True), jnp.int32(0), longer
    )
    filt_re, filt_im = second_section(part_re, part_im)
    next_local = regroup_next(next_inputs)
    next_re, next_im = spectrum(next_local, inner)
    out_re = next_re * filt_re - next_im * filt_im
    out_im = next_re * filt_im + next_im * filt_re
    final_re, final_im = back_section(out_re, out_im)
    result = last_rows(final_re, final_im, 0, half_rows, "rk,ckn->crn")
    result = result.reshape(1, channels, length).astype(jnp.bfloat16)
    next_out = lax.all_to_all(result, "ctx", split_axis=2, concat_axis=1, tiled=True)
    return (new_master, new_one, new_two, next_out)


def solution(mesh):
    return jax.shard_map(
        local,
        mesh=mesh,
        in_specs=(
            P("dp", None, "ctx"),
            P("dp", None, "ctx"),
            P("ctx", "dp"),
            P("ctx", "dp"),
            P("ctx", "dp"),
            P("dp", None, "ctx"),
        ),
        out_specs=(P("ctx", "dp"), P("ctx", "dp"), P("ctx", "dp"), P("dp", None, "ctx")),
        check_vma=False,
    )
```

profile of v0, /device:TPU:0, one launch (start us, length us, event | category | flops | bytes accessed | tf_op | source)
XLA Modules:
  0.0 735.0 jit_solution(11932400336401077649)
XLA Ops:
  9.2 2.1 reduce.8
  12.2 6.3 all-to-all-start.2
  20.0 2.1 reduce.7
  24.5 2.1 reduce.6
  27.5 2.1 fusion.113
  29.5 5.6 all-to-all-start.1
  38.1 2.3 convolution_negate_fusion.1
  40.4 3.2 fusion.52
  44.9 4.0 all-to-all-start
  49.9 2.6 bitcast_reduce_fusion.1
  55.3 4.2 convolution_negate_fusion.2
  59.5 4.2 fusion.54
  63.7 2.0 reshape.77
  65.8 2.6 bitcast_reduce_fusion.2
  71.1 3.2 convolution_negate_fusion.3
  74.4 3.2 fusion.56
  77.6 3.1 fusion.12
  80.7 3.1 fusion.16
  83.9 1.6 fusion.18
  85.5 1.8 fusion.22
  87.4 3.1 convolution_subtract_fusion.4
  90.5 3.1 convolution_add_fusion.4
  93.6 1.6 convolution_add_fusion.5
  95.3 1.8 multiply_subtract_fusion.3
  100.2 2.0 convolution_add_fusion.3
  103.8 2.6 fusion.34
  106.4 3.3 fusion.4
  109.8 2.6 fusion.6
  112.4 1.6 fusion.10
  114.0 2.8 convolution_add_fusion.2
  116.8 18.5 %reduce-scatter.2.cloned.1.call-done = bf16[64,2,256]{2,0,1:T(8,128)(2,1)} async-done(((bf16[256,2,256]{2,0,1:T(8,128)(2,1)}), bf16[64,2,256]{2,0,1:T(8,128)(2,1)}) %reduce-scatter.2.cloned.1.call-update) | async-done | bytes 65552 | tf_op jit(solution)/shard_map/reduce_scatter | solution.py:85
  137.5 9.3 %all_gather.3 = bf16[2,256,256]{2,1,0:T(8,128)(2,1)S(1)} all-gather(bf16[2,64,256]{2,1,0:T(8,128)(2,1)S(1)} %bitcast.192), channel_id=1, replica_groups=mesh['dp'=4,'ctx'=8] {'dp'}, dimensions={1}, use_global_device_ids=true | all-gather | bytes 327680 | tf_op jit(solution)/shard_map/all_gather | solution.py:101
  146.8 2.3 fusion
  149.1 2.3 convolution_bitcast_fusion
  151.3 1.7 fusion.98
  153.0 1.7 fusion.101
  154.7 1.7 convolution_subtract_fusion.1
  156.3 1.7 convolution_add_fusion.1
  158.0 3.5 multiply_add_fusion
  166.2 1.6 convolution_subtract_fusion
  167.8 2.8 fusion.27
  170.6 3.2 fusion.5
  174.0 50.3 %copy.63 = bf16[1,2,65536]{1,0,2:T(2,128)(2,1)} copy(bf16[1,2,65536]{2,1,0:T(2,128)(2,1)S(1)} %convert_element_type.177) | data formatting | bytes 524288 | tf_op jit(solution)/shard_map/convert_element_type | solution.py:110
  224.3 355.8 %reduce.9 = bf16[65536,2]{1,0:T(8,128)(2,1)} reduce(bf16[65536,1,2]{2,1,0:T(2,128)(2,1)} %bitcast.181, bf16[]{:T(256)} %broadcast.385), dimensions={1}, to_apply=%bitcast.143.reduce_sub_computation | reduce | bytes 524290
  580.1 31.5 %reshape.82 = bf16[8,2,8192]{2,1,0:T(2,128)(2,1)S(1)} reshape(bf16[65536,2]{1,0:T(8,128)(2,1)} %reduce.9) | data formatting | bytes 524288
  611.6 14.1 %all_to_all.63 = bf16[8,2,8192]{2,1,0:T(2,128)(2,1)S(1)} all-to-all(bf16[8,2,8192]{2,1,0:T(2,128)(2,1)S(1)} %reshape.82), channel_id=1, replica_groups=mesh['dp'=4,'ctx'=8] {'ctx'}, dimensions={0} | all-to-all | bytes 524288 | tf_op jit(solution)/shard_map/all_to_all | solution.py:111
  625.7 40.2 %reshape.83 = bf16[65536,1,2]{2,1,0:T(2,128)(2,1)} reshape(bf16[8,2,8192]{2,1,0:T(2,128)(2,1)S(1)} %all_to_all.63) | data formatting | bytes 524288
  665.9 60.8 %copy.64 = bf16[1,2,65536]{2,1,0:T(2,128)(2,1)S(1)} copy(bf16[1,2,65536]{1,0,2:T(2,128)(2,1)} %bitcast.182) | data formatting | bytes 524288 | tf_op jit(solution)/shard_map/all_to_all | solution.py:111
  (47 shorter events, 31.3 us)
Async XLA Ops:
  12.2 17.4 %all-to-all-start.2 = ((bf16[8,2,8192]{2,1,0:T(2,128)(2,1)}), bf16[8,2,8192]{2,1,0:T(2,128)(2,1)S(1)}, u32[]{:S(2)}, u32[]{:S(2)}) async-start(bf16[8,2,8192]{2,1,0:T(2,128)(2,1)} %reshape.80), calls=%async_computation.3 | async-start | bytes 524288 | tf_op jit(solution)/shard_map/all_to_all | solution.py:67
  29.5 15.3 %all-to-all-start.1 = ((bf16[8,2,8192]{2,1,0:T(2,128)(2,1)}), bf16[8,2,8192]{2,1,0:T(2,128)(2,1)S(1)}, u32[]{:S(2)}, u32[]{:S(2)}) async-start(bf16[8,2,8192]{2,1,0:T(2,128)(2,1)} %reshape.78), calls=%async_computation.1 | async-start | bytes 524288 | tf_op jit(solution)/shard_map/all_to_all | solution.py:74
  37.4 0.7 copy-start
  44.9 18.9 %all-to-all-start = ((bf16[8,2,8192]{2,1,0:T(2,128)(2,1)}), bf16[8,2,8192]{2,1,0:T(2,128)(2,1)}, u32[]{:S(2)}, u32[]{:S(2)}) async-start(bf16[8,2,8192]{2,1,0:T(2,128)(2,1)} %reshape.76), calls=%async_computation | async-start | bytes 524288 | tf_op jit(solution)/shard_map/all_to_all | solution.py:73
  48.9 86.4 %reduce-scatter.2.cloned.1.call-start = ((), (), s32[]{:S(2)}) async-start(), calls=%async_computation.5 | async-start | bytes 327680 | tf_op jit(solution)/shard_map/reduce_scatter | solution.py:85
  83.8 52.4 %copy-start.1 = (f32[2,16384]{1,0:T(2,128)S(1)}, f32[2,16384]{1,0:T(2,128)}, u32[]{:S(2)}) copy-start(f32[2,16384]{1,0:T(2,128)} %param.8) | copy-start | bytes 393220
  83.8 52.4 %copy-start.2 = (f32[2,16384]{1,0:T(2,128)S(1)}, f32[2,16384]{1,0:T(2,128)}, u32[]{:S(2)}) copy-start(f32[2,16384]{1,0:T(2,128)} %param.9) | copy-start | bytes 393220
  83.9 52.4 %copy-start.3 = (f32[2,16384]{1,0:T(2,128)S(1)}, f32[2,16384]{1,0:T(2,128)}, u32[]{:S(2)}) copy-start(f32[2,16384]{1,0:T(2,128)} %param.10) | copy-start | bytes 393220
Sparse Core Ops, SparseCore 0:
  109.9 25.3 reduce-scatter.1
where the time goes:
time: 744 us; the launch traced here: 735 us
  other arithmetic  366 us (49%)
  local copies, waits for them, and re-layouts  209 us (28%)
  matrix products  86.3 us (12%)
  blocking collectives  23.4 us (3%)
  waiting for transfers between devices  19.8 us (3%)
  starting transfers between devices  16 us (2%)
  between operations  14.7 us (2%)
    unnamed x5, other arithmetic  363 us
    dot_general x36, matrix products, mult(): jnp.einsum(form, left, right, precision=precise, preferred_element_type=j...  86.3 us
    unnamed x23, local copies, waits for them, and re-layouts  83.5 us
    all_to_all x3, local copies, waits for them, and re-layouts, local(): lax.all_to_all(result, 'ctx', split_axis=2, concat_axis=1, tiled=True)  61.9 us
    convert_element_type x3, local copies, waits for them, and re-layouts, local(): result = result.reshape(1, channels, length).astype(jnp.bfloat16)  50.5 us
    reduce_scatter x1, waiting for transfers between devices, local(): lax.psum_scatter(last_rows(back_re, back_im, jnp.int32(0), lax.axis_size(...  18.5 us
  transfers between devices with their start and end apart: 4, of which 2 were waited for; matrix products, arithmetic and copies ran while one was open for 5% of the time, Pallas kernels for 0%

commit v1 on v0

v1 whole, which is shorter than its diff:
```python
import functools

import jax
import jax.numpy as jnp
import numpy as np
from jax import lax
from jax.experimental import pallas as pl
from jax.experimental.pallas import tpu as pltpu
from jax.sharding import PartitionSpec as P

F32 = jnp.float32
BF16 = jnp.bfloat16
MESH = pl.DeviceIdType.MESH


def split_table(table):
    high = table.astype(np.float32).astype(jnp.bfloat16)
    low = (table - high.astype(np.float64)).astype(np.float32).astype(jnp.bfloat16)
    return high, low


def tables(rows, cols):
    length = rows * cols
    shifted = np.arange(rows, dtype=np.float64) + 0.25
    first = 2.0 * np.pi * np.outer(shifted, np.arange(rows)) / rows
    turn = 2.0 * np.pi * np.outer(shifted, np.arange(cols)) / length
    second = 2.0 * np.pi * (np.outer(np.arange(cols), np.arange(cols)) % cols) / cols
    in_first = np.concatenate([np.cos(first), -np.sin(first)], 0)
    out_last = np.concatenate([np.cos(first).T, -np.sin(first).T], 1) / length
    cosine, sine = np.cos(second), np.sin(second)
    forward = np.block([[cosine, -sine], [sine, cosine]])
    back = np.block([[cosine, sine], [-sine, cosine]])
    return (
        np.stack(split_table(in_first)),
        np.stack([np.cos(turn), -np.sin(turn)]).astype(np.float32),
        np.stack(split_table(forward)),
        np.stack(split_table(back)),
        np.stack(split_table(out_last)),
    )


def dot(left, right):
    return jnp.dot(left, right, preferred_element_type=F32)


def halves(value):
    high = value.astype(BF16)
    return high, (value - high.astype(F32)).astype(BF16)


def forward(block, t_first, t_turn, t_forward):
    rows, cols = block.shape
    mixed = dot(t_first[0], block) + dot(t_first[1], block)
    real, imag = mixed[:rows], mixed[rows:]
    turn_re, turn_im = t_turn[0], t_turn[1]
    turned = jnp.concatenate(
        [real * turn_re - imag * turn_im, real * turn_im + imag * turn_re], axis=1
    )
    high, low = halves(turned)
    spec = dot(high, t_forward[0]) + dot(low, t_forward[0]) + dot(high, t_forward[1])
    return spec[:, :cols], spec[:, cols:]


def inverse(real, imag, t_turn, t_back, t_last):
    cols = real.shape[1]
    high, low = halves(jnp.concatenate([real, imag], axis=1))
    mixed = dot(high, t_back[0]) + dot(low, t_back[0]) + dot(high, t_back[1])
    real, imag = mixed[:, :cols], mixed[:, cols:]
    turn_re, turn_im = t_turn[0], t_turn[1]
    high, low = halves(
        jnp.concatenate([real * turn_re + imag * turn_im, imag * turn_re - real * turn_im], axis=0)
    )
    return dot(t_last[0], high) + dot(t_last[0], low) + dot(t_last[1], high)


def layer(
    n_dp,
    n_ctx,
    x_hbm,
    g_hbm,
    master_hbm,
    one_hbm,
    two_hbm,
    n_hbm,
    first_hbm,
    turn_hbm,
    forward_hbm,
    back_hbm,
    last_hbm,
    master_out,
    one_out,
    two_out,
    next_out,
    raw,
    block_send,
    block_recv,
    t_first,
    t_turn,
    t_forward,
    t_back,
    t_last,
    state_in,
    state,
    state_out,
    spec,
    partial,
    grad_send,
    grad_recv,
    filt,
    out_send,
    out_recv,
    out_flat,
    local_sem,
    store_sem,
    block_ssem,
    block_rsem,
    grad_ssem,
    grad_rsem,
    filt_ssem,
    filt_rsem,
    out_ssem,
    out_rsem,
):
    me_dp = lax.axis_index("dp")
    me = lax.axis_index("ctx")
    channels = raw.shape[1]
    owned = block_recv.shape[1]
    rows_block, cols = block_send.shape[2:]
    rows = n_ctx * rows_block
    rows_own = filt.shape[2]

    barrier = pltpu.get_barrier_semaphore()

    def greet_ctx(i, carry):
        peer = lax.rem(me + i, n_ctx)
        pl.semaphore_signal(barrier, inc=1, device_id={"ctx": peer}, device_id_type=MESH)
        return carry

    def greet_dp(i, carry):
        peer = lax.rem(me_dp + i, n_dp)
        pl.semaphore_signal(barrier, inc=1, device_id={"dp": peer}, device_id_type=MESH)
        return carry

    lax.fori_loop(1, n_ctx, greet_ctx, 0)
    lax.fori_loop(1, n_dp, greet_dp, 0)

    loads = []
    for source, target in (
        (x_hbm.at[0], raw.at[0]),
        (g_hbm.at[0], raw.at[1]),
        (first_hbm, t_first),
        (turn_hbm, t_turn),
        (forward_hbm, t_forward),
        (back_hbm, t_back),
        (last_hbm, t_last),
        (n_hbm.at[0], raw.at[2]),
        (master_hbm, state_in.at[0]),
        (one_hbm, state_in.at[1]),
        (two_hbm, state_in.at[2]),
    ):
        copy = pltpu.make_async_copy(source, target, local_sem.at[len(loads)])
        copy.start()
        loads.append(copy)

    def regroup(which):
        block_send[which] = (
            raw[which].astype(F32).reshape(channels, rows_block, cols).astype(BF16)
        )

    def send_block(which, ch):
        def one(i, carry):
            peer = lax.rem(me + i, n_ctx)
            pltpu.make_async_remote_copy(
                src_ref=block_send.at[which, peer * owned + ch],
                dst_ref=block_recv.at[which, ch, me],
                send_sem=block_ssem.at[which, ch],
                recv_sem=block_rsem.at[which, ch],
                device_id={"ctx": peer},
                device_id_type=MESH,
            ).start()
            return carry

        lax.fori_loop(1, n_ctx, one, 0)
        block_recv[which, ch, me] = block_send[which, me * owned + ch]

    def wait_bytes(ref, count, sem):
        part = ref.at[pl.ds(0, count)]
        pltpu.make_async_copy(part, part, sem).wait()

    def wait_block(which, ch):
        wait_bytes(block_recv.at[which, ch], n_ctx - 1, block_rsem.at[which, ch])
        return block_recv[which, ch].reshape(rows, cols)

    def spectrum(block):
        return forward(block, t_first, t_turn, t_forward)

    loads[0].wait()
    regroup(0)
    pl.semaphore_wait(barrier, n_ctx + n_dp - 2)
    send_block(0, 0)
    loads[1].wait()
    regroup(1)
    send_block(1, 0)
    for ch in range(1, owned):
        send_block(0, ch)
        send_block(1, ch)
    for copy in loads[2:]:
        copy.wait()
    regroup(2)
    for which in range(3):
        for ch in range(owned):
            state[which, ch] = state_in[which, ch : ch + 1, :].reshape(rows_own, cols)

    def gradient(ch):
        spec[0], spec[1] = spectrum(wait_block(0, ch))
        g_block = wait_block(1, ch)
        if ch == owned - 1:
            for later in range(owned):
                send_block(2, later)
        g_re, g_im = spectrum(g_block)
        x_re, x_im = spec[0], spec[1]
        total = inverse(
            x_re * g_re + x_im * g_im, x_re * g_im - x_im * g_re, t_turn, t_back, t_last
        ).reshape(n_dp, rows_own, cols)
        partial[ch] = total
        grad_send[ch] = total.astype(BF16)

        def one(i, carry):
            peer = lax.rem(me_dp + i, n_dp)
            pltpu.make_async_remote_copy(
                src_ref=grad_send.at[ch, peer],
                dst_ref=grad_recv.at[ch, i - 1],
                send_sem=grad_ssem.at[ch],
                recv_sem=grad_rsem.at[ch],
                device_id={"dp": peer},
                device_id_type=MESH,
            ).start()
            return carry

        lax.fori_loop(1, n_dp, one, 0)

    def update(ch):
        wait_bytes(grad_recv.at[ch], n_dp - 1, grad_rsem.at[ch])
        grad = partial[ch, me_dp]
        for i in range(n_dp - 1):
            grad = grad + grad_recv[ch, i].astype(F32)
        master = state[0, ch]
        new_one = 0.9 * state[1, ch] + 0.1 * grad
        new_two = 0.999 * state[2, ch] + 0.001 * grad * grad
        first_hat = new_one / (1.0 - 0.9**10)
        second_hat = new_two / (1.0 - 0.999**10)
        new_master = master - 0.01 * (first_hat / (jnp.sqrt(second_hat) + 1e-08) + 0.1 * master)
        filt[ch, me_dp] = new_master.astype(BF16)

        def one(i, carry):
            peer = lax.rem(me_dp + i, n_dp)
            pltpu.make_async_remote_copy(
                src_ref=filt.at[ch, me_dp],
                dst_ref=filt.at[ch, me_dp],
                send_sem=filt_ssem.at[ch],
                recv_sem=filt_rsem.at[ch],
                device_id={"dp": peer},
                device_id_type=MESH,
            ).start()
            return carry

        lax.fori_loop(1, n_dp, one, 0)
        for which, value in enumerate((new_master, new_one, new_two)):
            state_out[which, ch : ch + 1, :] = value.reshape(1, rows_own * cols)

    def following(ch):
        spec[0], spec[1] = spectrum(wait_block(2, ch))
        wait_bytes(filt.at[ch], n_dp - 1, filt_rsem.at[ch])
        f_re, f_im = spectrum(filt[ch].reshape(rows, cols))
        x_re, x_im = spec[0], spec[1]
        result = inverse(
            x_re * f_re - x_im * f_im, x_re * f_im + x_im * f_re, t_turn, t_back, t_last
        )
        out_send[ch] = result.astype(BF16).reshape(n_ctx, rows_block, cols)

        def one(i, carry):
            peer = lax.rem(me + i, n_ctx)
            pltpu.make_async_remote_copy(
                src_ref=out_send.at[ch, peer],
                dst_ref=out_recv.at[me * owned + ch],
                send_sem=out_ssem.at[ch],
                recv_sem=out_rsem.at[ch],
                device_id={"ctx": peer},
                device_id_type=MESH,
            ).start()
            return carry

        lax.fori_loop(1, n_ctx, one, 0)
        out_recv[me * owned + ch] = out_send[ch, me]

    for ch in range(owned):
        gradient(ch)
        if ch:
            update(ch - 1)
    update(owned - 1)
    stores = []
    for which, target in enumerate((master_out, one_out, two_out)):
        copy = pltpu.make_async_copy(state_out.at[which], target, store_sem.at[which])
        copy.start()
        stores.append(copy)
    for ch in range(owned):
        following(ch)
    for ch in range(owned):
        wait_bytes(out_recv, n_ctx - 1, out_rsem.at[ch])
    out_flat[...] = out_recv[...].astype(F32).reshape(channels, rows_block * cols).astype(BF16)
    copy = pltpu.make_async_copy(out_flat, next_out.at[0], store_sem.at[3])
    copy.start()
    stores.append(copy)
    for ch in range(owned):
        for which in range(3):
            wait_bytes(block_send.at[which], n_ctx - 1, block_ssem.at[which, ch])
        wait_bytes(grad_send.at[ch], n_dp - 1, grad_ssem.at[ch])
        wait_bytes(filt.at[ch], n_dp - 1, filt_ssem.at[ch])
        wait_bytes(out_send.at[ch], n_ctx - 1, out_ssem.at[ch])
    for copy in stores:
        copy.wait()


def local(n_dp, n_ctx, inputs, out_grad, master, moment_one, moment_two, next_inputs):
    channels, span = inputs.shape[1:]
    owned, taps_own = master.shape
    length = n_ctx * span
    cols = min(256, span // 16)
    rows = length // cols
    rows_block, rows_own = span // cols, taps_own // cols
    table_list = tables(rows, cols)
    dma = pltpu.SemaphoreType.DMA
    vmem = pltpu.VMEM
    anywhere = pl.BlockSpec(memory_space=pl.ANY)
    macs = 12 * owned * length * (rows + 2 * cols) * 3
    return pl.pallas_call(
        functools.partial(layer, n_dp, n_ctx),
        name="layer",
        out_shape=(
            jax.ShapeDtypeStruct(master.shape, F32),
            jax.ShapeDtypeStruct(master.shape, F32),
            jax.ShapeDtypeStruct(master.shape, F32),
            jax.ShapeDtypeStruct(inputs.shape, BF16),
        ),
        in_specs=[anywhere] * 11,
        out_specs=[anywhere] * 4,
        scratch_shapes=[
            vmem((3, channels, span), BF16),
            vmem((3, channels, rows_block, cols), BF16),
            vmem((3, owned, n_ctx, rows_block, cols), BF16),
            *[vmem(table.shape, table.dtype) for table in table_list],
            vmem((3, owned, taps_own), F32),
            vmem((3, owned, rows_own, cols), F32),
            vmem((3, owned, taps_own), F32),
            vmem((2, rows, cols), F32),
            vmem((owned, n_dp, rows_own, cols), F32),
            vmem((owned, n_dp, rows_own, cols), BF16),
            vmem((owned, n_dp - 1, rows_own, cols), BF16),
            vmem((owned, n_dp, rows_own, cols), BF16),
            vmem((owned, n_ctx, rows_block, cols), BF16),
            vmem((channels, rows_block, cols), BF16),
            vmem((channels, span), BF16),
            dma((11,)),
            dma((4,)),
            dma((3, owned)),
            dma((3, owned)),
            dma((owned,)),
            dma((owned,)),
            dma((owned,)),
            dma((owned,)),
            dma((owned,)),
            dma((owned,)),
        ],
        compiler_params=pltpu.CompilerParams(
            collective_id=0, has_side_effects=True, vmem_limit_bytes=40 * 1024 * 1024
        ),
        cost_estimate=pl.CostEstimate(
            flops=2 * macs, bytes_accessed=8 * 1024 * 1024, transcendentals=0
        ),
    )(inputs, out_grad, master, moment_one, moment_two, next_inputs, *table_list)


def solution(mesh):
    return jax.shard_map(
        functools.partial(local, mesh.shape["dp"], mesh.shape["ctx"]),
        mesh=mesh,
        in_specs=(
            P("dp", None, "ctx"),
            P("dp", None, "ctx"),
            P("ctx", "dp"),
            P("ctx", "dp"),
            P("ctx", "dp"),
            P("dp", None, "ctx"),
        ),
        out_specs=(P("ctx", "dp"), P("ctx", "dp"), P("ctx", "dp"), P("dp", None, "ctx")),
        check_vma=False,
    )
```

time: 744 us -> 53.8 us (0.07); the launches traced: 735 us -> 53.3 us
  other arithmetic: 366 us -> 0 us
  local copies, waits for them, and re-layouts: 209 us -> 13.8 us
  matrix products: 86.3 us -> 0 us
  Pallas kernels: 0 us -> 38.9 us
  blocking collectives: 23.4 us -> 0 us
  waiting for transfers between devices: 19.8 us -> 0 us
  starting transfers between devices: 16 us -> 0 us
  between operations: 14.7 us -> 0.66 us
    unnamed x5 -> x0, other arithmetic: 363 us -> none
    dot_general x36 -> x0, matrix products: 86.3 us -> none  [mult(): jnp.einsum(form, left, right, precision=precise, preferred_element_type=j...]
    all_to_all x12 -> x0, local copies, waits for them, and re-layouts: 72.8 us -> none  [the longest x3 61.9 us: local(): lax.all_to_all(result, 'ctx', split_axis=2, concat_axis=1, tiled=True)]
    unnamed x23 -> x26, local copies, waits for them, and re-layouts: 83.5 us -> 13.8 us
    convert_element_type x3 -> x0, local copies, waits for them, and re-layouts: 50.5 us -> none  [local(): result = result.reshape(1, channels, length).astype(jnp.bfloat16)]
    pallas_call x0 -> x1, Pallas kernels: none -> 38.9 us  [local(): pl.pallas_call(functools.partial(layer, n_dp, n_ctx), name='layer', out_s...]
    reduce_scatter x1 -> x0, waiting for transfers between devices: 18.5 us -> none  [local(): lax.psum_scatter(last_rows(back_re, back_im, jnp.int32(0), lax.axis_size(...]
    all_to_all x3 -> x0, starting transfers between devices: 16 us -> none  [the longest x1 6.33 us: regroup_next(): lax.all_to_all(next_inputs, 'ctx', split_axis=1, concat_axis=2, tiled=True)]
  transfers between devices with their start and end apart: 4 -> 0, of which waited for: 2 -> 0; matrix products, arithmetic and copies ran while one was open for 5% -> 0% of each run, Pallas kernels for 0% -> 0%
where the time goes in v1:
time: 53.8 us; the launch traced here: 53.3 us
  Pallas kernels  38.9 us (72%)
  local copies, waits for them, and re-layouts  13.8 us (26%)
  between operations  0.66 us (1%)
    pallas_call x1, Pallas kernels, local(): pl.pallas_call(functools.partial(layer, n_dp, n_ctx), name='layer', out_s...  38.9 us
    unnamed x26, local copies, waits for them, and re-layouts  13.8 us

profile of v1, /device:TPU:0, one launch (start us, length us, event | category | flops | bytes accessed | tf_op | source)
XLA Modules:
  0.0 53.3 jit_solution(6230145674250854241)
XLA Ops:
  0.6 0.0 copy-start
  0.6 0.9 %copy-done = bf16[1,16,8192]{2,1,0:T(8,128)(2,1)S(1)} copy-done((bf16[1,16,8192]{2,1,0:T(8,128)(2,1)S(1)}, bf16[1,16,8192]{2,1,0:T(8,128)(2,1)}, u32[]{:S(2)}) %copy-start) | copy-done | bytes 262168
  1.6 0.0 copy-start.1
  1.6 0.9 %copy-done.1 = bf16[1,16,8192]{2,1,0:T(8,128)(2,1)S(1)} copy-done((bf16[1,16,8192]{2,1,0:T(8,128)(2,1)S(1)}, bf16[1,16,8192]{2,1,0:T(8,128)(2,1)}, u32[]{:S(2)}) %copy-start.1) | copy-done | bytes 262168
  2.5 0.0 copy-start.2
  2.5 0.9 %copy-done.2 = bf16[1,16,8192]{2,1,0:T(8,128)(2,1)S(1)} copy-done((bf16[1,16,8192]{2,1,0:T(8,128)(2,1)S(1)}, bf16[1,16,8192]{2,1,0:T(8,128)(2,1)}, u32[]{:S(2)}) %copy-start.2) | copy-done | bytes 262168
  3.5 0.0 copy-start.3
  3.5 0.9 %copy-done.3 = f32[2,16384]{1,0:T(2,128)S(1)} copy-done((f32[2,16384]{1,0:T(2,128)S(1)}, f32[2,16384]{1,0:T(2,128)}, u32[]{:S(2)}) %copy-start.3) | copy-done | bytes 131096
  4.4 0.0 copy-start.4
  4.4 0.9 %copy-done.4 = f32[2,16384]{1,0:T(2,128)S(1)} copy-done((f32[2,16384]{1,0:T(2,128)S(1)}, f32[2,16384]{1,0:T(2,128)}, u32[]{:S(2)}) %copy-start.4) | copy-done | bytes 131096
  5.3 0.0 copy-start.5
  5.3 0.9 %copy-done.5 = f32[2,16384]{1,0:T(2,128)S(1)} copy-done((f32[2,16384]{1,0:T(2,128)S(1)}, f32[2,16384]{1,0:T(2,128)}, u32[]{:S(2)}) %copy-start.5) | copy-done | bytes 131096
  6.2 0.0 copy-start.6
  6.2 1.2 %copy-done.6 = bf16[2,512,512]{2,1,0:T(8,128)(2,1)S(1)} copy-done((bf16[2,512,512]{2,1,0:T(8,128)(2,1)S(1)}, bf16[2,512,512]{2,1,0:T(8,128)(2,1)}, u32[]{:S(2)}) %copy-start.6) | copy-done | bytes 1048600
  7.4 0.0 copy-start.7
  7.4 1.2 %copy-done.7 = bf16[2,512,512]{2,1,0:T(8,128)(2,1)S(1)} copy-done((bf16[2,512,512]{2,1,0:T(8,128)(2,1)S(1)}, bf16[2,512,512]{2,1,0:T(8,128)(2,1)}, u32[]{:S(2)}) %copy-start.7) | copy-done | bytes 1048600
  8.6 0.0 copy-start.8
  8.7 1.0 %copy-done.8 = bf16[2,256,512]{2,1,0:T(8,128)(2,1)S(1)} copy-done((bf16[2,256,512]{2,1,0:T(8,128)(2,1)S(1)}, bf16[2,256,512]{2,1,0:T(8,128)(2,1)}, u32[]{:S(2)}) %copy-start.8) | copy-done | bytes 524312
  9.7 0.0 copy-start.9
  9.7 1.0 %copy-done.9 = f32[2,256,256]{2,1,0:T(8,128)S(1)} copy-done((f32[2,256,256]{2,1,0:T(8,128)S(1)}, f32[2,256,256]{2,1,0:T(8,128)}, u32[]{:S(2)}) %copy-start.9) | copy-done | bytes 524312
  10.7 0.0 copy-start.10
  10.7 1.0 %copy-done.10 = bf16[2,512,256]{2,1,0:T(8,128)(2,1)S(1)} copy-done((bf16[2,512,256]{2,1,0:T(8,128)(2,1)S(1)}, bf16[2,512,256]{2,1,0:T(8,128)(2,1)}, u32[]{:S(2)}) %copy-start.10) | copy-done | bytes 524312
  11.8 38.9 %layer.1 = (f32[2,16384]{1,0:T(2,128)S(1)}, f32[2,16384]{1,0:T(2,128)S(1)}, f32[2,16384]{1,0:T(2,128)S(1)}, bf16[1,16,8192]{2,1,0:T(8,128)(2,1)S(1)}) custom-call(bf16[1,16,8192]{2,1,0:T(8,128)(2,1)S(1)} %copy-done, bf16[1,16,8192]{2,1,0:T(8,128)(2,1)S(1)} %copy-done.1, f32[2,16384]{1,0:T(2,128)S(1)} %copy-done.3, f32[2,16384]{1,0:T(2,128)S(1)} %copy-done.4, ...), custom_call_target="tpu_custom_call" | custom-call | flops 7247757312 | bytes 8388608 | tf_op jit(solution)/shard_map/layer/pallas_call | solution.py:336
  50.7 0.7 %copy.19 = f32[2,16384]{1,0:T(2,128)} copy(f32[2,16384]{1,0:T(2,128)S(1)} %get-tuple-element.8) | data formatting | bytes 262144
  51.3 0.7 %copy.20 = f32[2,16384]{1,0:T(2,128)} copy(f32[2,16384]{1,0:T(2,128)S(1)} %get-tuple-element.9) | data formatting | bytes 262144
  52.0 0.7 %copy.21 = f32[2,16384]{1,0:T(2,128)} copy(f32[2,16384]{1,0:T(2,128)S(1)} %get-tuple-element.10) | data formatting | bytes 262144
  52.6 0.7 %copy.22 = bf16[1,16,8192]{2,1,0:T(8,128)(2,1)} copy(bf16[1,16,8192]{2,1,0:T(8,128)(2,1)S(1)} %get-tuple-element.11) | data formatting | bytes 524288
Async XLA Ops:
  0.6 1.0 %copy-start = (bf16[1,16,8192]{2,1,0:T(8,128)(2,1)S(1)}, bf16[1,16,8192]{2,1,0:T(8,128)(2,1)}, u32[]{:S(2)}) copy-start(bf16[1,16,8192]{2,1,0:T(8,128)(2,1)} %x_hbm.1) | copy-start | bytes 786436
  1.6 0.9 %copy-start.1 = (bf16[1,16,8192]{2,1,0:T(8,128)(2,1)S(1)}, bf16[1,16,8192]{2,1,0:T(8,128)(2,1)}, u32[]{:S(2)}) copy-start(bf16[1,16,8192]{2,1,0:T(8,128)(2,1)} %g_hbm.1) | copy-start | bytes 786436
  2.5 0.9 %copy-start.2 = (bf16[1,16,8192]{2,1,0:T(8,128)(2,1)S(1)}, bf16[1,16,8192]{2,1,0:T(8,128)(2,1)}, u32[]{:S(2)}) copy-start(bf16[1,16,8192]{2,1,0:T(8,128)(2,1)} %n_hbm.1) | copy-start | bytes 786436
  3.5 0.9 %copy-start.3 = (f32[2,16384]{1,0:T(2,128)S(1)}, f32[2,16384]{1,0:T(2,128)}, u32[]{:S(2)}) copy-start(f32[2,16384]{1,0:T(2,128)} %master_hbm.1) | copy-start | bytes 393220
  4.4 0.9 %copy-start.4 = (f32[2,16384]{1,0:T(2,128)S(1)}, f32[2,16384]{1,0:T(2,128)}, u32[]{:S(2)}) copy-start(f32[2,16384]{1,0:T(2,128)} %one_hbm.1) | copy-start | bytes 393220
  5.3 0.9 %copy-start.5 = (f32[2,16384]{1,0:T(2,128)S(1)}, f32[2,16384]{1,0:T(2,128)}, u32[]{:S(2)}) copy-start(f32[2,16384]{1,0:T(2,128)} %two_hbm.1) | copy-start | bytes 393220
  6.2 1.2 %copy-start.6 = (bf16[2,512,512]{2,1,0:T(8,128)(2,1)S(1)}, bf16[2,512,512]{2,1,0:T(8,128)(2,1)}, u32[]{:S(2)}) copy-start(bf16[2,512,512]{2,1,0:T(8,128)(2,1)} %constant.13.clone.back_hbm) | copy-start | bytes 3145732
  7.4 1.2 %copy-start.7 = (bf16[2,512,512]{2,1,0:T(8,128)(2,1)S(1)}, bf16[2,512,512]{2,1,0:T(8,128)(2,1)}, u32[]{:S(2)}) copy-start(bf16[2,512,512]{2,1,0:T(8,128)(2,1)} %constant.12.clone.forward_hbm) | copy-start | bytes 3145732
  8.6 1.0 %copy-start.8 = (bf16[2,256,512]{2,1,0:T(8,128)(2,1)S(1)}, bf16[2,256,512]{2,1,0:T(8,128)(2,1)}, u32[]{:S(2)}) copy-start(bf16[2,256,512]{2,1,0:T(8,128)(2,1)} %constant.14.clone.last_hbm) | copy-start | bytes 1572868
  9.7 1.0 %copy-start.9 = (f32[2,256,256]{2,1,0:T(8,128)S(1)}, f32[2,256,256]{2,1,0:T(8,128)}, u32[]{:S(2)}) copy-start(f32[2,256,256]{2,1,0:T(8,128)} %constant.11.clone.turn_hbm) | copy-start | bytes 1572868
  10.7 1.0 %copy-start.10 = (bf16[2,512,256]{2,1,0:T(8,128)(2,1)S(1)}, bf16[2,512,256]{2,1,0:T(8,128)(2,1)}, u32[]{:S(2)}) copy-start(bf16[2,512,256]{2,1,0:T(8,128)(2,1)} %constant.10.clone.first_hbm) | copy-start | bytes 1572868

commit v2 on v1

--- a/solution.py
+++ b/solution.py
@@ -13,29 +13,20 @@
 MESH = pl.DeviceIdType.MESH
 
 
-def split_table(table):
-    high = table.astype(np.float32).astype(jnp.bfloat16)
-    low = (table - high.astype(np.float64)).astype(np.float32).astype(jnp.bfloat16)
-    return high, low
-
-
 def tables(rows, cols):
     length = rows * cols
     shifted = np.arange(rows, dtype=np.float64) + 0.25
     first = 2.0 * np.pi * np.outer(shifted, np.arange(rows)) / rows
     turn = 2.0 * np.pi * np.outer(shifted, np.arange(cols)) / length
     second = 2.0 * np.pi * (np.outer(np.arange(cols), np.arange(cols)) % cols) / cols
-    in_first = np.concatenate([np.cos(first), -np.sin(first)], 0)
-    out_last = np.concatenate([np.cos(first).T, -np.sin(first).T], 1) / length
-    cosine, sine = np.cos(second), np.sin(second)
-    forward = np.block([[cosine, -sine], [sine, cosine]])
-    back = np.block([[cosine, sine], [-sine, cosine]])
-    return (
-        np.stack(split_table(in_first)),
-        np.stack([np.cos(turn), -np.sin(turn)]).astype(np.float32),
-        np.stack(split_table(forward)),
-        np.stack(split_table(back)),
-        np.stack(split_table(out_last)),
+    return tuple(
+        table.astype(np.float32)
+        for table in (
+            np.concatenate([np.cos(first), -np.sin(first)], 0),
+            np.stack([np.cos(turn), -np.sin(turn)]),
+            np.stack([np.cos(second), np.sin(second)]),
+            np.concatenate([np.cos(first).T, -np.sin(first).T], 1) / length,
+        )
     )
 
 
@@ -84,18 +75,20 @@
     n_hbm,
     first_hbm,
     turn_hbm,
-    forward_hbm,
-    back_hbm,
+    second_hbm,
     last_hbm,
     master_out,
     one_out,
     two_out,
-    next_out,
+    out_recv,
     raw,
     block_send,
     block_recv,
+    w_first,
+    t_turn,
+    w_second,
+    w_last,
     t_first,
-    t_turn,
     t_forward,
     t_back,
     t_last,
@@ -108,8 +101,6 @@
     grad_recv,
     filt,
     out_send,
-    out_recv,
-    out_flat,
     local_sem,
     store_sem,
     block_ssem,
@@ -148,11 +139,10 @@
     for source, target in (
         (x_hbm.at[0], raw.at[0]),
         (g_hbm.at[0], raw.at[1]),
-        (first_hbm, t_first),
+        (first_hbm, w_first),
         (turn_hbm, t_turn),
-        (forward_hbm, t_forward),
-        (back_hbm, t_back),
-        (last_hbm, t_last),
+        (second_hbm, w_second),
+        (last_hbm, w_last),
         (n_hbm.at[0], raw.at[2]),
         (master_hbm, state_in.at[0]),
         (one_hbm, state_in.at[1]),
@@ -206,13 +196,24 @@
         send_block(1, ch)
     for copy in loads[2:]:
         copy.wait()
+    t_first[0], t_first[1] = halves(w_first[...])
+    t_last[0], t_last[1] = halves(w_last[...])
+    low_cols, high_cols = slice(0, cols), slice(cols, 2 * cols)
+    for part, (cosine, sine) in enumerate(zip(halves(w_second[0]), halves(w_second[1]))):
+        for table, upper, lower in ((t_forward, -sine, sine), (t_back, sine, -sine)):
+            table[part, low_cols, low_cols] = cosine
+            table[part, low_cols, high_cols] = upper
+            table[part, high_cols, low_cols] = lower
+            table[part, high_cols, high_cols] = cosine
     regroup(2)
     for which in range(3):
         for ch in range(owned):
             state[which, ch] = state_in[which, ch : ch + 1, :].reshape(rows_own, cols)
 
+    def keep(values):
+        spec[0], spec[1] = values
+
     def gradient(ch):
-        spec[0], spec[1] = spectrum(wait_block(0, ch))
         g_block = wait_block(1, ch)
         if ch == owned - 1:
             for later in range(owned):
@@ -268,14 +269,14 @@
         for which, value in enumerate((new_master, new_one, new_two)):
             state_out[which, ch : ch + 1, :] = value.reshape(1, rows_own * cols)
 
-    def following(ch):
-        spec[0], spec[1] = spectrum(wait_block(2, ch))
+    def product(ch):
         wait_bytes(filt.at[ch], n_dp - 1, filt_rsem.at[ch])
         f_re, f_im = spectrum(filt[ch].reshape(rows, cols))
         x_re, x_im = spec[0], spec[1]
-        result = inverse(
-            x_re * f_re - x_im * f_im, x_re * f_im + x_im * f_re, t_turn, t_back, t_last
-        )
+        keep((x_re * f_re - x_im * f_im, x_re * f_im + x_im * f_re))
+
+    def finish(ch):
+        result = inverse(spec[0], spec[1], t_turn, t_back, t_last)
         out_send[ch] = result.astype(BF16).reshape(n_ctx, rows_block, cols)
 
         def one(i, carry):
@@ -291,34 +292,66 @@
             return carry
 
         lax.fori_loop(1, n_ctx, one, 0)
-        out_recv[me * owned + ch] = out_send[ch, me]
-
+        copy = pltpu.make_async_copy(
+            out_send.at[ch, me], out_recv.at[me * owned + ch], local_sem.at[ch]
+        )
+        copy.start()
+        stores.append(copy)
+
+    stores = []
     for ch in range(owned):
-        gradient(ch)
+        keep(spectrum(wait_block(0, ch)))
         if ch:
             update(ch - 1)
-    update(owned - 1)
-    stores = []
+        gradient(ch)
+    final = owned - 1
+    for ch in range(final):
+        keep(spectrum(wait_block(2, ch)))
+        product(ch)
+        if ch == final - 1:
+            update(final)
+        finish(ch)
+    if not final:
+        update(final)
+    keep(spectrum(wait_block(2, final)))
+    product(final)
     for which, target in enumerate((master_out, one_out, two_out)):
         copy = pltpu.make_async_copy(state_out.at[which], target, store_sem.at[which])
         copy.start()
         stores.append(copy)
-    for ch in range(owned):
-        following(ch)
-    for ch in range(owned):
-        wait_bytes(out_recv, n_ctx - 1, out_rsem.at[ch])
-    out_flat[...] = out_recv[...].astype(F32).reshape(channels, rows_block * cols).astype(BF16)
-    copy = pltpu.make_async_copy(out_flat, next_out.at[0], store_sem.at[3])
-    copy.start()
-    stores.append(copy)
+    finish(final)
     for ch in range(owned):
         for which in range(3):
             wait_bytes(block_send.at[which], n_ctx - 1, block_ssem.at[which, ch])
         wait_bytes(grad_send.at[ch], n_dp - 1, grad_ssem.at[ch])
         wait_bytes(filt.at[ch], n_dp - 1, filt_ssem.at[ch])
         wait_bytes(out_send.at[ch], n_ctx - 1, out_ssem.at[ch])
+    for ch in range(owned):
+        wait_bytes(out_recv, n_ctx - 1, out_rsem.at[ch])
     for copy in stores:
         copy.wait()
+
+
+def settle(states, blocks, states_out, next_out, block, flat, sems):
+    copies = [
+        pltpu.make_async_copy(source, target, sems.at[i])
+        for i, (source, target) in enumerate(zip(states, states_out))
+    ]
+    load = pltpu.make_async_copy(blocks, block, sems.at[3])
+    load.start()
+    for copy in copies:
+        copy.start()
+    load.wait()
+    flat[...] = block[...].astype(F32).reshape(flat.shape).astype(BF16)
+    store = pltpu.make_async_copy(flat, next_out.at[0], sems.at[4])
+    store.start()
+    store.wait()
+    for copy in copies:
+        copy.wait()
+
+
+def settle_kernel(master, one, two, blocks, master_out, one_out, two_out, next_out, *scratch):
+    settle((master, one, two), blocks, (master_out, one_out, two_out), next_out, *scratch)
 
 
 def local(n_dp, n_ctx, inputs, out_grad, master, moment_one, moment_two, next_inputs):
@@ -331,24 +364,28 @@
     table_list = tables(rows, cols)
     dma = pltpu.SemaphoreType.DMA
     vmem = pltpu.VMEM
-    anywhere = pl.BlockSpec(memory_space=pl.ANY)
+    anywhere = pl.BlockSpec(memory_space=pltpu.HBM)
     macs = 12 * owned * length * (rows + 2 * cols) * 3
-    return pl.pallas_call(
+    results = pl.pallas_call(
         functools.partial(layer, n_dp, n_ctx),
         name="layer",
         out_shape=(
             jax.ShapeDtypeStruct(master.shape, F32),
             jax.ShapeDtypeStruct(master.shape, F32),
             jax.ShapeDtypeStruct(master.shape, F32),
-            jax.ShapeDtypeStruct(inputs.shape, BF16),
+            jax.ShapeDtypeStruct((channels, rows_block, cols), BF16),
         ),
-        in_specs=[anywhere] * 11,
+        in_specs=[anywhere] * 10,
         out_specs=[anywhere] * 4,
         scratch_shapes=[
             vmem((3, channels, span), BF16),
             vmem((3, channels, rows_block, cols), BF16),
             vmem((3, owned, n_ctx, rows_block, cols), BF16),
-            *[vmem(table.shape, table.dtype) for table in table_list],
+            *[vmem(table.shape, F32) for table in table_list],
+            vmem((2, 2 * rows, rows), BF16),
+            vmem((2, 2 * cols, 2 * cols), BF16),
+            vmem((2, 2 * cols, 2 * cols), BF16),
+            vmem((2, rows, 2 * rows), BF16),
             vmem((3, owned, taps_own), F32),
             vmem((3, owned, rows_own, cols), F32),
             vmem((3, owned, taps_own), F32),
@@ -358,10 +395,8 @@
             vmem((owned, n_dp - 1, rows_own, cols), BF16),
             vmem((owned, n_dp, rows_own, cols), BF16),
             vmem((owned, n_ctx, rows_block, cols), BF16),
-            vmem((channels, rows_block, cols), BF16),
-            vmem((channels, span), BF16),
-            dma((11,)),
-            dma((4,)),
+            dma((10,)),
+            dma((3,)),
             dma((3, owned)),
             dma((3, owned)),
             dma((owned,)),
@@ -372,12 +407,30 @@
             dma((owned,)),
         ],
         compiler_params=pltpu.CompilerParams(
-            collective_id=0, has_side_effects=True, vmem_limit_bytes=40 * 1024 * 1024
+            collective_id=0, has_side_effects=True, vmem_limit_bytes=56 * 1024 * 1024
         ),
         cost_estimate=pl.CostEstimate(
             flops=2 * macs, bytes_accessed=8 * 1024 * 1024, transcendentals=0
         ),
     )(inputs, out_grad, master, moment_one, moment_two, next_inputs, *table_list)
+    return pl.pallas_call(
+        settle_kernel,
+        name="settle",
+        out_shape=(
+            jax.ShapeDtypeStruct(master.shape, F32),
+            jax.ShapeDtypeStruct(master.shape, F32),
+            jax.ShapeDtypeStruct(master.shape, F32),
+            jax.ShapeDtypeStruct(inputs.shape, BF16),
+        ),
+        in_specs=[anywhere] * 4,
+        out_specs=[anywhere] * 4,
+        scratch_shapes=[
+            vmem((channels, rows_block, cols), BF16),
+            vmem((channels, span), BF16),
+            dma((5,)),
+        ],
+        compiler_params=pltpu.CompilerParams(vmem_limit_bytes=56 * 1024 * 1024),
+    )(*results)
 
 
 def solution(mesh):

time: 53.8 us -> 55.1 us (1.024)
  Pallas kernels: 38.9 us -> 54.3 us
  local copies, waits for them, and re-layouts: 13.8 us -> 0 us
    unnamed x26 -> x0, local copies, waits for them, and re-layouts: 13.8 us -> none
    pallas_call x0 -> x1, Pallas kernels: none -> 13.1 us  [local(): pl.pallas_call(settle_kernel, name='settle', out_shape=(jax.ShapeDtypeStr...]
    pallas_call x1, Pallas kernels: 38.9 us -> 41.3 us  [local(): pl.pallas_call(functools.partial(layer, n_dp, n_ctx), name='layer', out_s...]
where the time goes in v2:
time: 55.1 us; the launch traced here: 55 us
  Pallas kernels  54.3 us (99%)
  between operations  0.64 us (1%)
    pallas_call x1, Pallas kernels, local(): pl.pallas_call(functools.partial(layer, n_dp, n_ctx), name='layer', out_s...  41.3 us
    pallas_call x1, Pallas kernels, local(): pl.pallas_call(settle_kernel, name='settle', out_shape=(jax.ShapeDtypeStr...  13.1 us

profile of v2, /device:TPU:0, one launch (start us, length us, event | category | flops | bytes accessed | tf_op | source)
XLA Modules:
  0.0 55.0 jit_solution(704062359140543908)
XLA Ops:
  0.6 41.3 %layer.1 = (f32[2,16384]{1,0:T(2,128)}, f32[2,16384]{1,0:T(2,128)}, f32[2,16384]{1,0:T(2,128)}, bf16[16,32,256]{2,1,0:T(8,128)(2,1)}) custom-call(bf16[1,16,8192]{2,1,0:T(8,128)(2,1)} %x_hbm.1, bf16[1,16,8192]{2,1,0:T(8,128)(2,1)} %g_hbm.1, f32[2,16384]{1,0:T(2,128)} %master_hbm.1, f32[2,16384]{1,0:T(2,128)} %one_hbm.1, f32[2,16384]{1,0:T(2,128)} %two_hbm.1, ...), custom_call_target="tpu_custom_call" | custom-call | flops 7247757312 | bytes 8388608 | tf_op jit(solution)/shard_map/layer/pallas_call | solution.py:369
  41.9 13.1 %settle.1 = (f32[2,16384]{1,0:T(2,128)}, f32[2,16384]{1,0:T(2,128)}, f32[2,16384]{1,0:T(2,128)}, bf16[1,16,8192]{2,1,0:T(8,128)(2,1)}) custom-call(f32[2,16384]{1,0:T(2,128)} %get-tuple-element.8.master, f32[2,16384]{1,0:T(2,128)} %get-tuple-element.9.one, f32[2,16384]{1,0:T(2,128)} %get-tuple-element.10.two, bf16[16,32,256]{2,1,0:T(8,128)(2,1)} %get-tuple-element.11.blocks), custom_call_target="tpu_custom_call" | custom-call | tf_op jit(solution)/shard_map/settle/pallas_call | solution.py:416

commit v3 on v2

--- a/solution.py
+++ b/solution.py
@@ -10,6 +10,7 @@
 
 F32 = jnp.float32
 BF16 = jnp.bfloat16
+LANES = 128
 MESH = pl.DeviceIdType.MESH
 
 
@@ -82,6 +83,7 @@
     two_out,
     out_recv,
     raw,
+    mixed,
     block_send,
     block_recv,
     w_first,
@@ -153,9 +155,17 @@
         loads.append(copy)
 
     def regroup(which):
-        block_send[which] = (
-            raw[which].astype(F32).reshape(channels, rows_block, cols).astype(BF16)
-        )
+        for i in range(rows_block):
+            part = raw[which, :, i * cols : (i + 1) * cols].astype(F32)
+            for lane in range(cols // LANES):
+                mixed[lane, i * channels : (i + 1) * channels, :] = part[
+                    :, lane * LANES : (lane + 1) * LANES
+                ]
+        for c in range(channels):
+            for lane in range(cols // LANES):
+                block_send[which, c, :, lane * LANES : (lane + 1) * LANES] = mixed[
+                    lane, pl.ds(c, rows_block, stride=channels), :
+                ].astype(BF16)
 
     def send_block(which, ch):
         def one(i, carry):
@@ -206,9 +216,15 @@
             table[part, high_cols, low_cols] = lower
             table[part, high_cols, high_cols] = cosine
     regroup(2)
-    for which in range(3):
-        for ch in range(owned):
-            state[which, ch] = state_in[which, ch : ch + 1, :].reshape(rows_own, cols)
+
+    def fold_row(i, carry):
+        span = pl.ds(pl.multiple_of(i * cols, LANES), cols)
+        for which in range(3):
+            for ch in range(owned):
+                state[which, ch, pl.ds(i, 1), :] = state_in[which, ch : ch + 1, span]
+        return carry
+
+    lax.fori_loop(0, rows_own, fold_row, 0, unroll=4)
 
     def keep(values):
         spec[0], spec[1] = values
@@ -267,7 +283,15 @@
 
         lax.fori_loop(1, n_dp, one, 0)
         for which, value in enumerate((new_master, new_one, new_two)):
-            state_out[which, ch : ch + 1, :] = value.reshape(1, rows_own * cols)
+            state[which, ch] = value
+
+        def flat_row(i, carry):
+            span = pl.ds(pl.multiple_of(i * cols, LANES), cols)
+            for which in range(3):
+                state_out[which, ch : ch + 1, span] = state[which, ch, pl.ds(i, 1), :]
+            return carry
+
+        lax.fori_loop(0, rows_own, flat_row, 0, unroll=8)
 
     def product(ch):
         wait_bytes(filt.at[ch], n_dp - 1, filt_rsem.at[ch])
@@ -332,26 +356,43 @@
         copy.wait()
 
 
-def settle(states, blocks, states_out, next_out, block, flat, sems):
-    copies = [
-        pltpu.make_async_copy(source, target, sems.at[i])
-        for i, (source, target) in enumerate(zip(states, states_out))
+def settle(
+    master, one, two, blocks, master_out, one_out, two_out, next_out, held, block, mixed, flat, sems
+):
+    channels, rows_block, cols = block.shape
+    load = pltpu.make_async_copy(blocks, block, sems.at[0])
+    load.start()
+    loads = [
+        pltpu.make_async_copy(source, held.at[i], sems.at[1 + i])
+        for i, source in enumerate((master, one, two))
     ]
-    load = pltpu.make_async_copy(blocks, block, sems.at[3])
-    load.start()
-    for copy in copies:
+    stores = [
+        pltpu.make_async_copy(held.at[i], target, sems.at[4 + i])
+        for i, target in enumerate((master_out, one_out, two_out))
+    ]
+    for copy in loads:
         copy.start()
     load.wait()
-    flat[...] = block[...].astype(F32).reshape(flat.shape).astype(BF16)
-    store = pltpu.make_async_copy(flat, next_out.at[0], sems.at[4])
+    for c in range(channels):
+        part = block[c].astype(F32)
+        for lane in range(cols // LANES):
+            mixed[lane, c * rows_block : (c + 1) * rows_block, :] = part[
+                :, lane * LANES : (lane + 1) * LANES
+            ]
+    for before, after in zip(loads, stores):
+        before.wait()
+        after.start()
+    for i in range(rows_block):
+        for lane in range(cols // LANES):
+            start = i * cols + lane * LANES
+            flat[:, start : start + LANES] = mixed[
+                lane, pl.ds(i, channels, stride=rows_block), :
+            ].astype(BF16)
+    store = pltpu.make_async_copy(flat, next_out.at[0], sems.at[7])
     store.start()
+    for copy in stores:
+        copy.wait()
     store.wait()
-    for copy in copies:
-        copy.wait()
-
-
-def settle_kernel(master, one, two, blocks, master_out, one_out, two_out, next_out, *scratch):
-    settle((master, one, two), blocks, (master_out, one_out, two_out), next_out, *scratch)
 
 
 def local(n_dp, n_ctx, inputs, out_grad, master, moment_one, moment_two, next_inputs):
@@ -379,6 +420,7 @@
         out_specs=[anywhere] * 4,
         scratch_shapes=[
             vmem((3, channels, span), BF16),
+            vmem((cols // LANES, channels * rows_block, LANES), F32),
             vmem((3, channels, rows_block, cols), BF16),
             vmem((3, owned, n_ctx, rows_block, cols), BF16),
             *[vmem(table.shape, F32) for table in table_list],
@@ -414,7 +456,7 @@
         ),
     )(inputs, out_grad, master, moment_one, moment_two, next_inputs, *table_list)
     return pl.pallas_call(
-        settle_kernel,
+        settle,
         name="settle",
         out_shape=(
             jax.ShapeDtypeStruct(master.shape, F32),
@@ -425,9 +467,11 @@
         in_specs=[anywhere] * 4,
         out_specs=[anywhere] * 4,
         scratch_shapes=[
+            vmem((3, owned, taps_own), F32),
             vmem((channels, rows_block, cols), BF16),
+            vmem((cols // LANES, channels * rows_block, LANES), F32),
             vmem((channels, span), BF16),
-            dma((5,)),
+            dma((8,)),
         ],
         compiler_params=pltpu.CompilerParams(vmem_limit_bytes=56 * 1024 * 1024),
     )(*results)

time: 55.1 us -> 45 us (0.82)
  Pallas kernels: 54.3 us -> 44.2 us
    pallas_call x1, Pallas kernels: 13.1 us -> 2.19 us  [local(): pl.pallas_call(settle, name='settle', out_shape=(jax.ShapeDtypeStruct(mas...]
    pallas_call x1, Pallas kernels: 41.3 us -> 42 us  [local(): pl.pallas_call(functools.partial(layer, n_dp, n_ctx), name='layer', out_s...]
where the time goes in v3:
time: 45 us; the launch traced here: 44.8 us
  Pallas kernels  44.2 us (98%)
  between operations  0.64 us (1%)
    pallas_call x1, Pallas kernels, local(): pl.pallas_call(functools.partial(layer, n_dp, n_ctx), name='layer', out_s...  42 us
    pallas_call x1, Pallas kernels, local(): pl.pallas_call(settle, name='settle', out_shape=(jax.ShapeDtypeStruct(mas...  2.19 us

profile of v3, /device:TPU:0, one launch (start us, length us, event | category | flops | bytes accessed | tf_op | source)
XLA Modules:
  0.0 44.8 jit_solution(14659111376686034783)
XLA Ops:
  0.6 42.0 %layer.1 = (f32[2,16384]{1,0:T(2,128)}, f32[2,16384]{1,0:T(2,128)}, f32[2,16384]{1,0:T(2,128)}, bf16[16,32,256]{2,1,0:T(8,128)(2,1)}) custom-call(bf16[1,16,8192]{2,1,0:T(8,128)(2,1)} %x_hbm.1, bf16[1,16,8192]{2,1,0:T(8,128)(2,1)} %g_hbm.1, f32[2,16384]{1,0:T(2,128)} %master_hbm.1, f32[2,16384]{1,0:T(2,128)} %one_hbm.1, f32[2,16384]{1,0:T(2,128)} %two_hbm.1, ...), custom_call_target="tpu_custom_call" | custom-call | flops 7247757312 | bytes 8388608 | tf_op jit(solution)/shard_map/layer/pallas_call | solution.py:410
  42.6 2.2 %settle.1 = (f32[2,16384]{1,0:T(2,128)}, f32[2,16384]{1,0:T(2,128)}, f32[2,16384]{1,0:T(2,128)}, bf16[1,16,8192]{2,1,0:T(8,128)(2,1)}) custom-call(f32[2,16384]{1,0:T(2,128)} %get-tuple-element.8.master, f32[2,16384]{1,0:T(2,128)} %get-tuple-element.9.one, f32[2,16384]{1,0:T(2,128)} %get-tuple-element.10.two, bf16[16,32,256]{2,1,0:T(8,128)(2,1)} %get-tuple-element.11.blocks), custom_call_target="tpu_custom_call" | custom-call | tf_op jit(solution)/shard_map/settle/pallas_call | solution.py:458

commit v4 on v3

--- a/solution.py
+++ b/solution.py
@@ -201,9 +201,6 @@
     loads[1].wait()
     regroup(1)
     send_block(1, 0)
-    for ch in range(1, owned):
-        send_block(0, ch)
-        send_block(1, ch)
     for copy in loads[2:]:
         copy.wait()
     t_first[0], t_first[1] = halves(w_first[...])
@@ -231,9 +228,7 @@
 
     def gradient(ch):
         g_block = wait_block(1, ch)
-        if ch == owned - 1:
-            for later in range(owned):
-                send_block(2, later)
+        send_block(*((1, ch + 1) if ch + 1 < owned else (2, 0)))
         g_re, g_im = spectrum(g_block)
         x_re, x_im = spec[0], spec[1]
         total = inverse(
@@ -324,12 +319,16 @@
 
     stores = []
     for ch in range(owned):
-        keep(spectrum(wait_block(0, ch)))
+        x_block = wait_block(0, ch)
+        if ch + 1 < owned:
+            send_block(0, ch + 1)
+        keep(spectrum(x_block))
         if ch:
             update(ch - 1)
         gradient(ch)
     final = owned - 1
     for ch in range(final):
+        send_block(2, ch + 1)
         keep(spectrum(wait_block(2, ch)))
         product(ch)
         if ch == final - 1:

time: 45 us -> 40.6 us (0.902)
  Pallas kernels: 44.2 us -> 39.8 us
    pallas_call x1, Pallas kernels: 42 us -> 37.6 us  [local(): pl.pallas_call(functools.partial(layer, n_dp, n_ctx), name='layer', out_s...]
where the time goes in v4:
time: 40.6 us; the launch traced here: 40.4 us
  Pallas kernels  39.8 us (98%)
  between operations  0.64 us (2%)
    pallas_call x1, Pallas kernels, local(): pl.pallas_call(functools.partial(layer, n_dp, n_ctx), name='layer', out_s...  37.6 us
    pallas_call x1, Pallas kernels, local(): pl.pallas_call(settle, name='settle', out_shape=(jax.ShapeDtypeStruct(mas...  2.19 us

profile of v4, /device:TPU:0, one launch (start us, length us, event | category | flops | bytes accessed | tf_op | source)
XLA Modules:
  0.0 40.4 jit_solution(8940369167501647565)
XLA Ops:
  0.6 37.6 %layer.1 = (f32[2,16384]{1,0:T(2,128)}, f32[2,16384]{1,0:T(2,128)}, f32[2,16384]{1,0:T(2,128)}, bf16[16,32,256]{2,1,0:T(8,128)(2,1)}) custom-call(bf16[1,16,8192]{2,1,0:T(8,128)(2,1)} %x_hbm.1, bf16[1,16,8192]{2,1,0:T(8,128)(2,1)} %g_hbm.1, f32[2,16384]{1,0:T(2,128)} %master_hbm.1, f32[2,16384]{1,0:T(2,128)} %one_hbm.1, f32[2,16384]{1,0:T(2,128)} %two_hbm.1, ...), custom_call_target="tpu_custom_call" | custom-call | flops 7247757312 | bytes 8388608 | tf_op jit(solution)/shard_map/layer/pallas_call | solution.py:409
  38.3 2.2 %settle.1 = (f32[2,16384]{1,0:T(2,128)}, f32[2,16384]{1,0:T(2,128)}, f32[2,16384]{1,0:T(2,128)}, bf16[1,16,8192]{2,1,0:T(8,128)(2,1)}) custom-call(f32[2,16384]{1,0:T(2,128)} %get-tuple-element.8.master, f32[2,16384]{1,0:T(2,128)} %get-tuple-element.9.one, f32[2,16384]{1,0:T(2,128)} %get-tuple-element.10.two, bf16[16,32,256]{2,1,0:T(8,128)(2,1)} %get-tuple-element.11.blocks), custom_call_target="tpu_custom_call" | custom-call | tf_op jit(solution)/shard_map/settle/pallas_call | solution.py:457

commit v5 on v4

--- a/solution.py
+++ b/solution.py
@@ -40,29 +40,37 @@
     return high, (value - high.astype(F32)).astype(BF16)
 
 
+def thrice(value, table):
+    rows = value.shape[0]
+    high, low = halves(value)
+    both = dot(jnp.concatenate([high, low], axis=0), table[0])
+    return both[:rows] + (both[rows:] + dot(high, table[1]))
+
+
 def forward(block, t_first, t_turn, t_forward):
     rows, cols = block.shape
-    mixed = dot(t_first[0], block) + dot(t_first[1], block)
-    real, imag = mixed[:rows], mixed[rows:]
+    mixed = dot(t_first[...], block)
+    real = mixed[:rows] + mixed[2 * rows : 3 * rows]
+    imag = mixed[rows : 2 * rows] + mixed[3 * rows :]
     turn_re, turn_im = t_turn[0], t_turn[1]
     turned = jnp.concatenate(
         [real * turn_re - imag * turn_im, real * turn_im + imag * turn_re], axis=1
     )
-    high, low = halves(turned)
-    spec = dot(high, t_forward[0]) + dot(low, t_forward[0]) + dot(high, t_forward[1])
+    spec = thrice(turned, t_forward)
     return spec[:, :cols], spec[:, cols:]
 
 
 def inverse(real, imag, t_turn, t_back, t_last):
     cols = real.shape[1]
-    high, low = halves(jnp.concatenate([real, imag], axis=1))
-    mixed = dot(high, t_back[0]) + dot(low, t_back[0]) + dot(high, t_back[1])
+    rows = real.shape[0]
+    mixed = thrice(jnp.concatenate([real, imag], axis=1), t_back)
     real, imag = mixed[:, :cols], mixed[:, cols:]
     turn_re, turn_im = t_turn[0], t_turn[1]
     high, low = halves(
         jnp.concatenate([real * turn_re + imag * turn_im, imag * turn_re - real * turn_im], axis=0)
     )
-    return dot(t_last[0], high) + dot(t_last[0], low) + dot(t_last[1], high)
+    both = dot(t_last[...], high)
+    return both[:rows] + (both[rows:] + dot(t_last[:rows], low))
 
 
 def layer(
@@ -203,8 +211,8 @@
     send_block(1, 0)
     for copy in loads[2:]:
         copy.wait()
-    t_first[0], t_first[1] = halves(w_first[...])
-    t_last[0], t_last[1] = halves(w_last[...])
+    t_first[: 2 * rows], t_first[2 * rows :] = halves(w_first[...])
+    t_last[:rows], t_last[rows:] = halves(w_last[...])
     low_cols, high_cols = slice(0, cols), slice(cols, 2 * cols)
     for part, (cosine, sine) in enumerate(zip(halves(w_second[0]), halves(w_second[1]))):
         for table, upper, lower in ((t_forward, -sine, sine), (t_back, sine, -sine)):
@@ -423,10 +431,10 @@
             vmem((3, channels, rows_block, cols), BF16),
             vmem((3, owned, n_ctx, rows_block, cols), BF16),
             *[vmem(table.shape, F32) for table in table_list],
-            vmem((2, 2 * rows, rows), BF16),
+            vmem((4 * rows, rows), BF16),
             vmem((2, 2 * cols, 2 * cols), BF16),
             vmem((2, 2 * cols, 2 * cols), BF16),
-            vmem((2, rows, 2 * rows), BF16),
+            vmem((2 * rows, 2 * rows), BF16),
             vmem((3, owned, taps_own), F32),
             vmem((3, owned, rows_own, cols), F32),
             vmem((3, owned, taps_own), F32),

time: 40.6 us -> 39.3 us (0.968)
  Pallas kernels: 39.8 us -> 38.5 us
    pallas_call x1, Pallas kernels: 37.6 us -> 36.3 us  [local(): pl.pallas_call(functools.partial(layer, n_dp, n_ctx), name='layer', out_s...]
where the time goes in v5:
time: 39.3 us; the launch traced here: 39.2 us
  Pallas kernels  38.5 us (98%)
  between operations  0.64 us (2%)
    pallas_call x1, Pallas kernels, local(): pl.pallas_call(functools.partial(layer, n_dp, n_ctx), name='layer', out_s...  36.3 us
    pallas_call x1, Pallas kernels, local(): pl.pallas_call(settle, name='settle', out_shape=(jax.ShapeDtypeStruct(mas...  2.19 us

profile of v5, /device:TPU:0, one launch (start us, length us, event | category | flops | bytes accessed | tf_op | source)
XLA Modules:
  0.0 39.2 jit_solution(904691743897810382)
XLA Ops:
  0.6 36.3 %layer.1 = (f32[2,16384]{1,0:T(2,128)}, f32[2,16384]{1,0:T(2,128)}, f32[2,16384]{1,0:T(2,128)}, bf16[16,32,256]{2,1,0:T(8,128)(2,1)}) custom-call(bf16[1,16,8192]{2,1,0:T(8,128)(2,1)} %x_hbm.1, bf16[1,16,8192]{2,1,0:T(8,128)(2,1)} %g_hbm.1, f32[2,16384]{1,0:T(2,128)} %master_hbm.1, f32[2,16384]{1,0:T(2,128)} %one_hbm.1, f32[2,16384]{1,0:T(2,128)} %two_hbm.1, ...), custom_call_target="tpu_custom_call" | custom-call | flops 7247757312 | bytes 8388608 | tf_op jit(solution)/shard_map/layer/pallas_call | solution.py:417
  37.0 2.2 %settle.1 = (f32[2,16384]{1,0:T(2,128)}, f32[2,16384]{1,0:T(2,128)}, f32[2,16384]{1,0:T(2,128)}, bf16[1,16,8192]{2,1,0:T(8,128)(2,1)}) custom-call(f32[2,16384]{1,0:T(2,128)} %get-tuple-element.8.master, f32[2,16384]{1,0:T(2,128)} %get-tuple-element.9.one, f32[2,16384]{1,0:T(2,128)} %get-tuple-element.10.two, bf16[16,32,256]{2,1,0:T(8,128)(2,1)} %get-tuple-element.11.blocks), custom_call_target="tpu_custom_call" | custom-call | tf_op jit(solution)/shard_map/settle/pallas_call | solution.py:465

commit v6 on v5

--- a/solution.py
+++ b/solution.py
@@ -47,24 +47,27 @@
     return both[:rows] + (both[rows:] + dot(high, table[1]))
 
 
-def forward(block, t_first, t_turn, t_forward):
-    rows, cols = block.shape
+def columns(real, imag, t_second, back):
+    common = thrice(real + imag, t_second.at[0])
+    if back:
+        return common - thrice(imag, t_second.at[2]), common + thrice(real, t_second.at[1])
+    return common + thrice(imag, t_second.at[1]), common - thrice(real, t_second.at[2])
+
+
+def forward(block, t_first, t_turn, t_second):
+    rows = block.shape[0]
     mixed = dot(t_first[...], block)
     real = mixed[:rows] + mixed[2 * rows : 3 * rows]
     imag = mixed[rows : 2 * rows] + mixed[3 * rows :]
     turn_re, turn_im = t_turn[0], t_turn[1]
-    turned = jnp.concatenate(
-        [real * turn_re - imag * turn_im, real * turn_im + imag * turn_re], axis=1
+    return columns(
+        real * turn_re - imag * turn_im, real * turn_im + imag * turn_re, t_second, False
     )
-    spec = thrice(turned, t_forward)
-    return spec[:, :cols], spec[:, cols:]
-
-
-def inverse(real, imag, t_turn, t_back, t_last):
-    cols = real.shape[1]
+
+
+def inverse(real, imag, t_turn, t_second, t_last):
     rows = real.shape[0]
-    mixed = thrice(jnp.concatenate([real, imag], axis=1), t_back)
-    real, imag = mixed[:, :cols], mixed[:, cols:]
+    real, imag = columns(real, imag, t_second, True)
     turn_re, turn_im = t_turn[0], t_turn[1]
     high, low = halves(
         jnp.concatenate([real * turn_re + imag * turn_im, imag * turn_re - real * turn_im], axis=0)
@@ -99,8 +102,7 @@
     w_second,
     w_last,
     t_first,
-    t_forward,
-    t_back,
+    t_second,
     t_last,
     state_in,
     state,
@@ -132,6 +134,10 @@
 
     barrier = pltpu.get_barrier_semaphore()
 
+    def partner(i):
+        offset = n_ctx // 2 + lax.div(i, 2) * (2 * lax.rem(i, 2) - 1)
+        return lax.rem(me + offset, n_ctx)
+
     def greet_ctx(i, carry):
         peer = lax.rem(me + i, n_ctx)
         pl.semaphore_signal(barrier, inc=1, device_id={"ctx": peer}, device_id_type=MESH)
@@ -177,7 +183,7 @@
 
     def send_block(which, ch):
         def one(i, carry):
-            peer = lax.rem(me + i, n_ctx)
+            peer = partner(i)
             pltpu.make_async_remote_copy(
                 src_ref=block_send.at[which, peer * owned + ch],
                 dst_ref=block_recv.at[which, ch, me],
@@ -200,7 +206,7 @@
         return block_recv[which, ch].reshape(rows, cols)
 
     def spectrum(block):
-        return forward(block, t_first, t_turn, t_forward)
+        return forward(block, t_first, t_turn, t_second)
 
     loads[0].wait()
     regroup(0)
@@ -213,13 +219,9 @@
         copy.wait()
     t_first[: 2 * rows], t_first[2 * rows :] = halves(w_first[...])
     t_last[:rows], t_last[rows:] = halves(w_last[...])
-    low_cols, high_cols = slice(0, cols), slice(cols, 2 * cols)
-    for part, (cosine, sine) in enumerate(zip(halves(w_second[0]), halves(w_second[1]))):
-        for table, upper, lower in ((t_forward, -sine, sine), (t_back, sine, -sine)):
-            table[part, low_cols, low_cols] = cosine
-            table[part, low_cols, high_cols] = upper
-            table[part, high_cols, low_cols] = lower
-            table[part, high_cols, high_cols] = cosine
+    cosine, sine = w_second[0], w_second[1]
+    for i, table in enumerate((cosine, sine - cosine, sine + cosine)):
+        t_second[i, 0], t_second[i, 1] = halves(table)
     regroup(2)
 
     def fold_row(i, carry):
@@ -240,7 +242,7 @@
         g_re, g_im = spectrum(g_block)
         x_re, x_im = spec[0], spec[1]
         total = inverse(
-            x_re * g_re + x_im * g_im, x_re * g_im - x_im * g_re, t_turn, t_back, t_last
+            x_re * g_re + x_im * g_im, x_re * g_im - x_im * g_re, t_turn, t_second, t_last
         ).reshape(n_dp, rows_own, cols)
         partial[ch] = total
         grad_send[ch] = total.astype(BF16)
@@ -303,11 +305,11 @@
         keep((x_re * f_re - x_im * f_im, x_re * f_im + x_im * f_re))
 
     def finish(ch):
-        result = inverse(spec[0], spec[1], t_turn, t_back, t_last)
+        result = inverse(spec[0], spec[1], t_turn, t_second, t_last)
         out_send[ch] = result.astype(BF16).reshape(n_ctx, rows_block, cols)
 
         def one(i, carry):
-            peer = lax.rem(me + i, n_ctx)
+            peer = partner(i)
             pltpu.make_async_remote_copy(
                 src_ref=out_send.at[ch, peer],
                 dst_ref=out_recv.at[me * owned + ch],
@@ -432,8 +434,7 @@
             vmem((3, owned, n_ctx, rows_block, cols), BF16),
             *[vmem(table.shape, F32) for table in table_list],
             vmem((4 * rows, rows), BF16),
-            vmem((2, 2 * cols, 2 * cols), BF16),
-            vmem((2, 2 * cols, 2 * cols), BF16),
+            vmem((3, 2, cols, cols), BF16),
             vmem((2 * rows, 2 * rows), BF16),
             vmem((3, owned, taps_own), F32),
             vmem((3, owned, rows_own, cols), F32),

time: 39.3 us -> 39.9 us (1.015)
  Pallas kernels: 38.5 us -> 39.1 us
    pallas_call x1, Pallas kernels: 36.3 us -> 36.9 us  [local(): pl.pallas_call(functools.partial(layer, n_dp, n_ctx), name='layer', out_s...]
where the time goes in v6:
time: 39.9 us; the launch traced here: 39.7 us
  Pallas kernels  39.1 us (98%)
  between operations  0.64 us (2%)
    pallas_call x1, Pallas kernels, local(): pl.pallas_call(functools.partial(layer, n_dp, n_ctx), name='layer', out_s...  36.9 us
    pallas_call x1, Pallas kernels, local(): pl.pallas_call(settle, name='settle', out_shape=(jax.ShapeDtypeStruct(mas...  2.19 us

profile of v6, /device:TPU:0, one launch (start us, length us, event | category | flops | bytes accessed | tf_op | source)
XLA Modules:
  0.0 39.7 jit_solution(9133279208424939222)
XLA Ops:
  0.6 36.9 %layer.1 = (f32[2,16384]{1,0:T(2,128)}, f32[2,16384]{1,0:T(2,128)}, f32[2,16384]{1,0:T(2,128)}, bf16[16,32,256]{2,1,0:T(8,128)(2,1)}) custom-call(bf16[1,16,8192]{2,1,0:T(8,128)(2,1)} %x_hbm.1, bf16[1,16,8192]{2,1,0:T(8,128)(2,1)} %g_hbm.1, f32[2,16384]{1,0:T(2,128)} %master_hbm.1, f32[2,16384]{1,0:T(2,128)} %one_hbm.1, f32[2,16384]{1,0:T(2,128)} %two_hbm.1, ...), custom_call_target="tpu_custom_call" | custom-call | flops 7247757312 | bytes 8388608 | tf_op jit(solution)/shard_map/layer/pallas_call | solution.py:419
  37.5 2.2 %settle.1 = (f32[2,16384]{1,0:T(2,128)}, f32[2,16384]{1,0:T(2,128)}, f32[2,16384]{1,0:T(2,128)}, bf16[1,16,8192]{2,1,0:T(8,128)(2,1)}) custom-call(f32[2,16384]{1,0:T(2,128)} %get-tuple-element.8.master, f32[2,16384]{1,0:T(2,128)} %get-tuple-element.9.one, f32[2,16384]{1,0:T(2,128)} %get-tuple-element.10.two, bf16[16,32,256]{2,1,0:T(8,128)(2,1)} %get-tuple-element.11.blocks), custom_call_target="tpu_custom_call" | custom-call | tf_op jit(solution)/shard_map/settle/pallas_call | solution.py:466
